TPU v7x, 32 devices: a whole 2x2x4 slice. The times are simulated.
32 devices in a mesh: groups: 2 (over y), fsdp: 4 (over z), sub: 2 (over x), rep: 2 (over core).
Axes of the slice: x: 2, y: 2, z: 4, core: 2. Of those that a mesh axis runs over, the one named last changes fastest.
Arguments:
- activations: bfloat16 [6144, 8192], P(('groups', 'fsdp', 'rep'), 'sub'), parts along dimension 0, may hold values from -6 to 6
- cotangent: bfloat16 [6144, 1024], P(('groups', 'fsdp', 'rep'), 'sub'), parts along dimension 0, may hold values from -6 to 6
- base_weight: bfloat16 [1024, 8192], P('fsdp', 'sub'), may hold values from -0.0625 to 0.0625
- adapter_down: bfloat16 [16, 8192, 64], P(('groups', 'fsdp'), 'sub'), parts along dimension 0, may hold values from -0.0625 to 0.0625
- adapter_up: bfloat16 [16, 64, 1024], P(('groups', 'fsdp'), None, 'sub'), parts along dimension 0, may hold values from -0.75 to 0.75
- tile_counts: int32 [16], P('groups'), parts along dimension 0, may hold values from 1 to 3, as said below
- tile_length: int32 [48], P(('groups', 'fsdp', 'rep')), parts along dimension 0, may hold values from 1 to 128
- tile_adapter: int32 [48], P(('groups', 'fsdp', 'rep')), parts along dimension 0, may hold values from 0 to 1
Outputs:
- value_proj: bfloat16 [6144, 1024], P(('groups', 'fsdp', 'rep'), 'sub'), parts along dimension 0
- input_grad: bfloat16 [6144, 8192], P(('groups', 'fsdp', 'rep'), 'sub'), parts along dimension 0
- down_grad: bfloat16 [16, 8192, 64], P(('groups', 'fsdp'), 'sub'), parts along dimension 0
- up_grad: bfloat16 [16, 64, 1024], P(('groups', 'fsdp'), None, 'sub'), parts along dimension 0
There are 2 independent parts, one for each index of `groups`. A program takes and returns all parts, laid end to end along the dimension named above; an argument that names none is the same for every part. Nothing has to cross between parts.
Inputs may be any that keep to these rules, and one draw needn't show every extreme that they name: tile_counts[f * 2 + r] is the number of leading slots in use at fsdp index f and rep index r; the two counts of one fsdp index add up to at most 4, and 3 occurs in every draw.
All inputs are finite; a program needn't handle non-finite values.
Results may differ from a plain program's by a relative error of at most 0.0049.
Values may be sent and summed in bfloat16 or wider, within the bound.
A program may use at most 64 MiB of HBM per device.

v0:
```python
import jax
import jax.numpy as jnp
from jax import lax
from jax.sharding import PartitionSpec as P

adapter_scale = 2.0


def on_device(
    activations,
    cotangent,
    base_weight,
    adapter_down,
    adapter_up,
    tile_counts,
    tile_length,
    tile_adapter,
):
    slot_count = tile_length.shape[0]
    tile_rows = activations.shape[0] // slot_count
    feat_width = activations.shape[1]
    head_width = cotangent.shape[1]
    own_sets = adapter_down.shape[0]
    low_rank = adapter_down.shape[2]
    rep_count = lax.axis_size("rep")
    fsdp_pos = lax.axis_index("fsdp")
    rep_pos = lax.axis_index("rep")
    own_count = tile_counts[fsdp_pos * rep_count + rep_pos]
    slot_ids = jnp.arange(slot_count, dtype=jnp.int32)
    positions = jnp.arange(tile_rows, dtype=jnp.int32)
    row_valid = (
        (slot_ids < own_count)[:, None] & (positions[None, :] < tile_length[:, None])
    ).astype(jnp.bfloat16)
    masked_dy = cotangent.reshape(slot_count, tile_rows, head_width) * row_valid[:, :, None]
    adapter_pick = (tile_adapter[:, None] == jnp.arange(own_sets, dtype=jnp.int32)[None, :]).astype(
        jnp.bfloat16
    )
    contract_last = (((1,), (1,)), ((), ()))
    contract_first = (((0,), (0,)), ((), ()))
    valid_rows = row_valid.reshape(-1)[:, None].astype(jnp.float32)
    work_dy = masked_dy.reshape(-1, head_width)
    row_count = activations.shape[0]
    set_count = adapter_down.shape[0]
    chosen_rows = jnp.broadcast_to(
        adapter_pick[:, None, :], (adapter_pick.shape[0], tile_rows, set_count)
    ).reshape(row_count, set_count)
    flattened_down = adapter_down.transpose(1, 0, 2).reshape(feat_width, set_count * low_rank)
    flat_up = adapter_up.reshape(set_count * low_rank, head_width)
    pick_adapter_rows = chosen_rows.astype(jnp.float32)[:, :, None]
    adapter_input_grad = jnp.dot(
        activations, flattened_down, preferred_element_type=jnp.float32
    ).reshape(row_count, set_count, low_rank)
    adapter_backward = lax.dot_general(
        work_dy, flat_up, contract_last, preferred_element_type=jnp.float32
    ).reshape(row_count, set_count, low_rank)
    input_piece = jnp.sum(adapter_input_grad * pick_adapter_rows, axis=1)
    backward_piece = jnp.sum(adapter_backward * pick_adapter_rows, axis=1)
    in_sum, back_sum = lax.psum((input_piece, backward_piece), "sub")
    in_low = in_sum.astype(jnp.bfloat16)
    back_low = back_sum.astype(jnp.bfloat16)
    in_wide = (chosen_rows[:, :, None] * in_low[:, None, :]).reshape(
        row_count, set_count * low_rank
    )
    back_wide = (chosen_rows[:, :, None] * back_low[:, None, :]).reshape(
        row_count, set_count * low_rank
    )
    full_dy = lax.all_gather(work_dy, "sub", axis=1, tiled=True)
    whole_weight = lax.all_gather(base_weight, "fsdp", axis=0, tiled=True)
    value_part = lax.dot_general(
        activations, whole_weight, contract_last, preferred_element_type=jnp.float32
    )
    input_frozen_grad = jnp.dot(full_dy, whole_weight, preferred_element_type=jnp.float32)
    value_frozen_out = lax.psum_scatter(value_part, "sub", scatter_dimension=1, tiled=True)
    value_total_out = value_frozen_out + adapter_scale * jnp.dot(
        in_wide, flat_up, preferred_element_type=jnp.float32
    )
    input_total_grad = input_frozen_grad + adapter_scale * lax.dot_general(
        back_wide, flattened_down, contract_last, preferred_element_type=jnp.float32
    )
    down_product = adapter_scale * lax.dot_general(
        activations, back_wide, contract_first, preferred_element_type=jnp.float32
    )
    up_product = adapter_scale * lax.dot_general(
        in_wide, work_dy, contract_first, preferred_element_type=jnp.float32
    )
    down_product = down_product.reshape(feat_width, set_count, low_rank).transpose(1, 0, 2)
    up_product = up_product.reshape(set_count, low_rank, head_width)
    value_total_out, input_total_grad, down_grad, up_grad = (
        value_total_out,
        input_total_grad,
        down_product,
        up_product,
    )
    down_total, up_total = lax.psum((down_grad, up_grad), "rep")
    value_proj = (value_total_out * valid_rows).astype(jnp.bfloat16)
    return (
        value_proj,
        input_total_grad.astype(jnp.bfloat16),
        down_total.astype(jnp.bfloat16),
        up_total.astype(jnp.bfloat16),
    )


def solution(mesh):
    return jax.shard_map(
        on_device,
        mesh=mesh,
        in_specs=(
            P(("groups", "fsdp", "rep"), "sub"),
            P(("groups", "fsdp", "rep"), "sub"),
            P("fsdp", "sub"),
            P(("groups", "fsdp"), "sub", None),
            P(("groups", "fsdp"), None, "sub"),
            P("groups"),
            P(("groups", "fsdp", "rep")),
            P(("groups", "fsdp", "rep")),
        ),
        out_specs=(
            P(("groups", "fsdp", "rep"), "sub"),
            P(("groups", "fsdp", "rep"), "sub"),
            P(("groups", "fsdp"), "sub", None),
            P(("groups", "fsdp"), None, "sub"),
        ),
        check_vma=False,
    )
```

profile of v0, /device:TPU:2, one launch (start us, length us, event | category | flops | bytes accessed | tf_op | source)
XLA Modules:
  0.0 199.9 jit_solution(8999345675580186445)
XLA Ops:
  7.2 0.0 copy-start
  7.2 0.0 all-gather.2.cloned.1.call-start
  7.2 0.7 all-gather.2.cloned.1.call-update
  7.9 0.0 reduce-scatter.2.cloned.1.call-start
  8.0 0.8 compare_convert_fusion
  8.8 0.1 broadcast_bitcast_fusion
  8.9 0.2 copy-done
  9.1 3.0 %fusion.11 = f32[384,64]{0,1:T(8,128)} fusion(bf16[384,4096]{1,0:T(8,128)(2,1)S(1)} %copy-done, bf16[2,4096,64]{1,2,0:T(8,128)(2,1)} %param.11, f32[384,2]{0,1:T(2,128)S(1)} %get-tuple-element.8), kind=kOutput, calls=%fused_computation.14 | convolution fusion | flops 402726912 | bytes 4295680 | tf_op jit(solution)/shard_map/dot_general | solution.py:50
  12.0 0.0 copy-done.7
  12.0 0.6 dynamic_slice.3
  12.6 0.6 iota_compare_fusion.1
  13.3 0.0 copy-done.6
  13.3 0.1 fusion.22
  13.3 1.1 broadcast_multiply_fusion
  14.5 1.8 fusion.14
  16.3 10.5 %all-reduce.4 = (bf16[384,64]{0,1:T(8,128)(2,1)}, bf16[384,64]{0,1:T(8,128)(2,1)}) all-reduce(f32[384,64]{0,1:T(8,128)} %fusion.11, f32[384,64]{0,1:T(8,128)} %fusion.14), channel_id=1, replica_groups=mesh['groups'=2,'fsdp'=4,'sub'=2,'rep'=2] {'sub'}, use_global_device_ids=true, to_apply=%region_2.0 | all-reduce | flops 49152 | bytes 294912 | tf_op jit(solution)/shard_map/psum | solution.py:58
  26.8 0.8 broadcast_multiply_fusion.2
  27.6 2.0 %convolution_multiply_fusion = f32[128,4096]{1,0:T(8,128)} fusion(bf16[384,128]{0,1:T(8,128)(2,1)S(1)} %bitcast.69, bf16[384,4096]{1,0:T(8,128)(2,1)S(1)} %copy-done), kind=kOutput, calls=%fused_computation.3 | convolution fusion | flops 403177472 | bytes 5341184 | tf_op jit(solution)/shard_map/dot_general | solution.py:80
  29.6 0.9 convolution_multiply_fusion.1
  30.6 10.6 %all_gather.7 = bf16[384,1024]{1,0:T(8,128)(2,1)} all-gather(bf16[384,512]{1,0:T(8,128)(2,1)S(1)} %broadcast_multiply_fusion), channel_id=1, replica_groups=mesh['groups'=2,'fsdp'=4,'sub'=2,'rep'=2] {'sub'}, dimensions={1}, use_global_device_ids=true | all-gather | bytes 1179648 | tf_op jit(solution)/shard_map/all_gather | solution.py:67
  41.2 119.3 %all-gather.2.cloned.1.call-done = bf16[1024,4096]{1,0:T(8,128)(2,1)} async-done(((bf16[256,4096]{1,0:T(8,128)(2,1)}), bf16[1024,4096]{1,0:T(8,128)(2,1)}) %all-gather.2.cloned.1.call-update) | async-done | bytes 8388624 | tf_op jit(solution)/shard_map/all_gather | solution.py:68
  160.5 7.1 %fusion.24 = f32[384,1024]{1,0:T(8,128)} fusion(bf16[384,4096]{1,0:T(8,128)(2,1)S(1)} %copy-done, bf16[1024,4096]{1,0:T(8,128)(2,1)} %all-gather.2.cloned.1.call-done), kind=kOutput, calls=%fused_computation.32 | convolution fusion | flops 3221225472 | bytes 13107200 | tf_op jit(solution)/shard_map/dot_general | solution.py:69
  167.6 0.0 reduce-scatter.2.cloned.1.call-update
  167.6 0.0 copy-done.1
  167.6 10.5 %all-reduce.5 = (bf16[2,4096,64]{1,2,0:T(8,128)(2,1)}, bf16[2,64,512]{2,1,0:T(8,128)(2,1)}) all-reduce(f32[2,4096,64]{1,2,0:T(8,128)} %bitcast.66, f32[2,64,512]{2,1,0:T(8,128)S(1)} %bitcast.67), channel_id=1, replica_groups=mesh['groups'=2,'fsdp'=4,'sub'=2,'rep'=2] {'rep'}, use_global_device_ids=true, to_apply=%region_5.0 | all-reduce | flops 589824 | bytes 3538944 | tf_op jit(solution)/shard_map/psum | solution.py:94
  178.1 6.1 %fusion.25 = f32[384,4096]{1,0:T(8,128)S(1)} fusion(bf16[384,1024]{1,0:T(8,128)(2,1)} %all_gather.7, bf16[1024,4096]{1,0:T(8,128)(2,1)} %all-gather.2.cloned.1.call-done), kind=kOutput, calls=%fused_computation.33 | convolution fusion | flops 3221225472 | bytes 15466496 | tf_op jit(solution)/shard_map/dot_general | solution.py:72
  184.2 0.0 copy-done.2
  184.2 0.0 copy-start.3
  184.2 2.7 %fusion.1 = bf16[384,4096]{1,0:T(8,128)(2,1)} fusion(f32[384,4096]{1,0:T(8,128)S(1)} %fusion.25, bf16[2,4096,64]{1,2,0:T(8,128)(2,1)S(1)} %copy-done.2, bf16[384,64]{0,1:T(8,128)(2,1)S(1)} %copy-done.4, bf16[384,2]{0,1:T(2,128)(2,1)S(1)} %get-tuple-element.9), kind=kOutput, calls=%fused_computation.2 | convolution fusion | flops 407420928 | bytes 10536448 | tf_op jit(solution)/shard_map/dot_general | solution.py:77
  186.9 4.0 %reduce-scatter.2.cloned.1.call-done = f32[384,512]{1,0:T(8,128)} async-done(((f32[384,1024]{1,0:T(8,128)}), f32[384,512]{1,0:T(8,128)}) %reduce-scatter.2.cloned.1.call-update) | async-done | bytes 786448 | tf_op jit(solution)/shard_map/reduce_scatter | solution.py:73
  190.9 0.0 copy-done.3
  190.9 2.2 %fusion.7 = bf16[384,512]{1,0:T(8,128)(2,1)} fusion(f32[384,512]{1,0:T(8,128)} %reduce-scatter.2.cloned.1.call-done, bf16[2,64,512]{2,1,0:T(8,128)(2,1)S(1)} %copy-done.3, f32[384]{0:T(512)S(1)} %get-tuple-element.10, bf16[384,64]{0,1:T(8,128)(2,1)S(1)} %copy-done.5, bf16[384,2]{0,1:T(2,128)(2,1)S(1)} %get-tuple-element.9), kind=kOutput, calls=%fused_computation.10 | convolution fusion | flops 51167232 | bytes 1362944 | tf_op jit(solution)/shard_map/dot_general | solution.py:74
  (9 shorter events, 0.0 us)
Async XLA Ops:
  7.2 1.9 copy-start
  7.2 153.3 %all-gather.2.cloned.1.call-start = ((), (), s32[]{:S(2)}) async-start(), calls=%async_computation.1 | async-start | bytes 10485760 | tf_op jit(solution)/shard_map/all_gather | solution.py:68
  7.9 183.0 %reduce-scatter.2.cloned.1.call-start = ((), (), s32[]{:S(2)}) async-start(), calls=%async_computation.2 | async-start | bytes 2359296 | tf_op jit(solution)/shard_map/reduce_scatter | solution.py:73
  9.1 3.0 %copy-start.7 = (s32[8]{0:T(128)S(1)}, s32[8]{0:T(128)}, u32[]{:S(2)}) copy-start(s32[8]{0:T(128)} %param.13) | copy-start | bytes 100
  9.1 4.2 %copy-start.6 = (s32[3]{0:T(128)S(1)}, s32[3]{0:T(128)}, u32[]{:S(2)}) copy-start(s32[3]{0:T(128)} %param.14) | copy-start | bytes 40
  41.2 126.4 %copy-start.1 = (f32[128,512]{1,0:T(8,128)S(1)}, f32[128,512]{1,0:T(8,128)}, u32[]{:S(2)}) copy-start(f32[128,512]{1,0:T(8,128)} %convolution_multiply_fusion.1) | copy-start | bytes 786436
  178.1 6.1 %copy-start.2 = (bf16[2,4096,64]{1,2,0:T(8,128)(2,1)S(1)}, bf16[2,4096,64]{1,2,0:T(8,128)(2,1)}, u32[]{:S(2)}) copy-start(bf16[2,4096,64]{1,2,0:T(8,128)(2,1)} %param.11) | copy-start | bytes 3145732
  178.1 6.1 %copy-start.4 = (bf16[384,64]{0,1:T(8,128)(2,1)S(1)}, bf16[384,64]{0,1:T(8,128)(2,1)}, u32[]{:S(2)}) copy-start(bf16[384,64]{0,1:T(8,128)(2,1)} %get-tuple-element.7) | copy-start | bytes 147460
  184.2 6.7 %copy-start.3 = (bf16[2,64,512]{2,1,0:T(8,128)(2,1)S(1)}, bf16[2,64,512]{2,1,0:T(8,128)(2,1)}, u32[]{:S(2)}) copy-start(bf16[2,64,512]{2,1,0:T(8,128)(2,1)} %param.12) | copy-start | bytes 393220
  184.2 6.6 %copy-start.5 = (bf16[384,64]{0,1:T(8,128)(2,1)S(1)}, bf16[384,64]{0,1:T(8,128)(2,1)}, u32[]{:S(2)}) copy-start(bf16[384,64]{0,1:T(8,128)(2,1)} %get-tuple-element.6) | copy-start | bytes 147460
Sparse Core Ops, SparseCore 0:
  9.6 150.8 all-gather.1
  167.7 23.1 reduce-scatter.1
where the time goes:
time: 203 us; the launch traced here: 200 us
  waiting for transfers between devices  124 us (61%)
  blocking collectives  31.5 us (16%)
  matrix products  25.8 us (13%)
  between operations  14.1 us (7%)
  other arithmetic  3.5 us (2%)
    all_gather x1, waiting for transfers between devices, on_device(): whole_weight = lax.all_gather(base_weight, 'fsdp', axis=0, tiled=True)  119 us
    all_gather x1, blocking collectives, on_device(): full_dy = lax.all_gather(work_dy, 'sub', axis=1, tiled=True)  10.6 us
    psum x1, blocking collectives, on_device(): down_total, up_total = lax.psum((down_grad, up_grad), 'rep')  10.5 us
    psum x1, blocking collectives, on_device(): in_sum, back_sum = lax.psum((input_piece, backward_piece), 'sub')  10.5 us
    dot_general x1, matrix products, on_device(): lax.dot_general(activations, whole_weight, contract_last, preferred_eleme...  7.07 us
    dot_general x1, matrix products, on_device(): jnp.dot(full_dy, whole_weight, preferred_element_type=jnp.float32)  6.1 us
  transfers between devices with their start and end apart: 2, of which 2 were waited for; matrix products, arithmetic and copies ran while one was open for 10% of the time, Pallas kernels for 0%

commit v1 on v0

--- a/solution.py
+++ b/solution.py
@@ -1,12 +1,16 @@
+import functools
+
 import jax
 import jax.numpy as jnp
 from jax import lax
+from jax.experimental import pallas as pl
+from jax.experimental.pallas import tpu as pltpu
 from jax.sharding import PartitionSpec as P
 
 adapter_scale = 2.0
 
 
-def on_device(
+def on_device_general(
     activations,
     cotangent,
     base_weight,
@@ -101,9 +105,472 @@
     )
 
 
+CHUNKS = 4
+NT = (((1,), (1,)), ((), ()))
+
+
+def dot_nt(a, b):
+    return lax.dot_general(a, b, NT, preferred_element_type=jnp.float32)
+
+
+def dot_nn(a, b):
+    return jnp.dot(a, b, preferred_element_type=jnp.float32)
+
+
+def fused_kernel(
+    counts,
+    lengths,
+    picks,
+    act_h,
+    dy_h,
+    w_h,
+    down_h,
+    up_h,
+    value_h,
+    igrad_h,
+    dgrad_h,
+    ugrad_h,
+    act,
+    dy_raw,
+    dy_blocks,
+    weights,
+    down,
+    up,
+    low,
+    in_wide,
+    back_wide,
+    dpart,
+    dsum,
+    upart,
+    usum,
+    vpart,
+    vsend,
+    vrecv,
+    vout,
+    igacc,
+    igout,
+    local_sem,
+    out_sem,
+    own_send,
+    z_send,
+    z_recv,
+    y_send,
+    y_recv,
+    ca_send,
+    ca_recv,
+    cb_send,
+    cb_recv,
+    x_send,
+    x_recv,
+    v_send,
+    v_recv,
+    r_send,
+    r_recv,
+):
+    g = lax.axis_index("groups")
+    f = lax.axis_index("fsdp")
+    s = lax.axis_index("sub")
+    r = lax.axis_index("rep")
+    fsdp = 4
+    slots = lengths.shape[0]
+    rows, feats = act.shape
+    tile = rows // slots
+    block = w_h.shape[0]
+    quarter = feats // 4
+    width = quarter // CHUNKS
+    to_y = {"groups": 1 - g}
+    to_x = {"sub": 1 - s}
+    to_r = {"rep": 1 - r}
+    to_lo = {"fsdp": jnp.maximum(f - 1, 0)}
+    to_hi = {"fsdp": jnp.minimum(f + 1, fsdp - 1)}
+
+    barrier = pltpu.get_barrier_semaphore()
+    for peer in (to_y, to_x, to_r):
+        pl.semaphore_signal(barrier, inc=1, device_id=peer, device_id_type=pl.DeviceIdType.MESH)
+
+    @pl.when(f > 0)
+    def _():
+        pl.semaphore_signal(barrier, inc=1, device_id=to_lo, device_id_type=pl.DeviceIdType.MESH)
+
+    @pl.when(f < fsdp - 1)
+    def _():
+        pl.semaphore_signal(barrier, inc=1, device_id=to_hi, device_id_type=pl.DeviceIdType.MESH)
+
+    local = [
+        pltpu.make_async_copy(src, dst, local_sem.at[i])
+        for i, (src, dst) in enumerate(
+            (
+                (act_h, act),
+                (down_h, down),
+                (w_h, weights.at[f]),
+                (dy_h, dy_raw.at[s]),
+                (up_h, up.at[s]),
+            )
+        )
+    ]
+    for copy in local:
+        copy.start()
+    ends = jnp.where(f == 0, 1, 0) + jnp.where(f == fsdp - 1, 1, 0)
+    pl.semaphore_wait(barrier, 5 - ends)
+
+    def remote(src, dst, send, recv, peer):
+        return pltpu.make_async_remote_copy(
+            src_ref=src,
+            dst_ref=dst,
+            send_sem=send,
+            recv_sem=recv,
+            device_id=peer,
+            device_id_type=pl.DeviceIdType.MESH,
+        )
+
+    def columns(gg, rr, c):
+        return pl.ds(pl.multiple_of((gg * 2 + rr) * quarter + c * width, width), width)
+
+    def own_copy(c, down_way):
+        cols = columns(g, r, c)
+        return remote(
+            w_h.at[:, cols],
+            weights.at[f, :, cols],
+            own_send.at[0 if down_way else 1, c],
+            z_recv.at[f, c],
+            to_lo if down_way else to_hi,
+        )
+
+    for c in range(CHUNKS):
+
+        @pl.when(f > 0)
+        def _():
+            own_copy(c, True).start()
+
+        @pl.when(f < fsdp - 1)
+        def _():
+            own_copy(c, False).start()
+
+    x_dy = remote(dy_h, dy_raw.at[s], x_send.at[0], x_recv.at[0], to_x)
+    x_up = remote(up_h, up.at[s], x_send.at[1], x_recv.at[1], to_x)
+    x_low = remote(low.at[s], low.at[s], x_send.at[2], x_recv.at[2], to_x)
+    x_up.start()
+    x_dy.start()
+
+    order = ((1, 2, 3), (2, 0, 3), (1, 3, 0), (2, 1, 0))
+    arrivals = []
+    for t in range(fsdp - 1):
+        j = jnp.int32(order[0][t])
+        for p in range(1, fsdp):
+            j = jnp.where(f == p, order[p][t], j)
+        arrivals.append(j)
+
+    def piece(j, gg, rr, c):
+        return weights.at[j, :, columns(gg, rr, c)]
+
+    def z_copy(j, c, peer):
+        here = piece(j, g, r, c)
+        return remote(here, here, z_send.at[j, c], z_recv.at[j, c], peer)
+
+    def y_copy(j, c):
+        here = piece(j, g, r, c)
+        return remote(here, here, y_send.at[j, c], y_recv.at[j, c], to_y)
+
+    def ca_copy(j, c):
+        here = piece(j, g, r, c)
+        return remote(here, here, ca_send.at[j, c], ca_recv.at[j, c], to_r)
+
+    def cb_copy(j, c):
+        here = piece(j, 1 - g, r, c)
+        return remote(here, here, cb_send.at[j, c], cb_recv.at[j, c], to_r)
+
+    def step(i):
+        j, c = arrivals[i // CHUNKS], i % CHUNKS
+        z_copy(j, c, to_y).wait_recv()
+
+        @pl.when((j > f) & (f > 0))
+        def _():
+            z_copy(j, c, to_lo).start()
+
+        @pl.when((j < f) & (f < fsdp - 1))
+        def _():
+            z_copy(j, c, to_hi).start()
+
+        y_copy(j, c).start()
+        ca_copy(j, c).start()
+
+    def y_step(i):
+        j, c = arrivals[i // CHUNKS], i % CHUNKS
+        here = piece(j, 1 - g, r, c)
+        remote(here, here, y_send.at[j, c], y_recv.at[j, c], to_y).wait_recv()
+        cb_copy(j, c).start()
+
+    def both(i):
+        step(i)
+        y_step(i - 1)
+
+    def core_wait(t):
+        j = arrivals[t]
+        for c in range(CHUNKS):
+            here = piece(j, g, 1 - r, c)
+            remote(here, here, ca_send.at[j, c], ca_recv.at[j, c], to_r).wait_recv()
+            here = piece(j, 1 - g, 1 - r, c)
+            remote(here, here, cb_send.at[j, c], cb_recv.at[j, c], to_r).wait_recv()
+
+    own_count = counts[f * 2 + r]
+
+    def valid(i, lanes):
+        used = jnp.where(i < own_count, lengths[i], 0)
+        return lax.broadcasted_iota(jnp.int32, (tile, lanes), 0) < used
+
+    def chosen(i):
+        lanes = lax.broadcasted_iota(jnp.int32, (tile, down.shape[0]), 1)
+        return lanes // (down.shape[0] // 2) == picks[i]
+
+    def tiles(i):
+        return slice(i * tile, (i + 1) * tile)
+
+    def v_copy(q):
+        return remote(vsend.at[q], vrecv.at[q], v_send.at[q], v_recv.at[q], to_x)
+
+    def value_block(j):
+        part = dot_nt(act[...], weights[j])
+        vpart[j] = part
+
+        @pl.when(j // 2 != s)
+        def _():
+            q = j % 2
+            vsend[q] = part.astype(jnp.bfloat16)
+            v_copy(q).start()
+
+    step_cols = 512
+
+    def grad_block(j):
+        @pl.loop(0, feats // step_cols)
+        def _(k):
+            cols = pl.ds(pl.multiple_of(k * step_cols, step_cols), step_cols)
+            igacc[:, cols] += dot_nn(dy_blocks[j], weights[j, :, cols])
+
+    local[0].wait()
+    local[1].wait()
+    wide = dot_nt(act[...], down[...])
+    for i in range(slots):
+        low[s, tiles(i), :] = jnp.where(chosen(i), wide[tiles(i), :], 0.0)
+    x_low.start()
+    local[2].wait()
+    value_block(f)
+    step(0)
+    both(1)
+    local[3].wait()
+    local[4].wait()
+    x_dy_in = remote(dy_raw.at[1 - s], dy_raw.at[1 - s], x_send.at[0], x_recv.at[0], to_x)
+    x_up_in = remote(up.at[1 - s], up.at[1 - s], x_send.at[1], x_recv.at[1], to_x)
+    x_low_in = remote(low.at[1 - s], low.at[1 - s], x_send.at[2], x_recv.at[2], to_x)
+    x_dy_in.wait_recv()
+    x_up_in.wait_recv()
+    for h in range(2):
+        for q in range(2):
+            for i in range(slots):
+                raw = dy_raw[h, tiles(i), q * block : (q + 1) * block].astype(jnp.float32)
+                dy_blocks[2 * h + q, tiles(i), :] = jnp.where(valid(i, block), raw, 0.0).astype(
+                    jnp.bfloat16
+                )
+    both(2)
+    back = dot_nt(dy_blocks[0], up[0, :, 0:block])
+    for b in range(1, 4):
+        q = b % 2
+        back += dot_nt(dy_blocks[b], up[b // 2, :, q * block : (q + 1) * block])
+    back = jnp.concatenate(
+        [jnp.where(chosen(i), back[tiles(i), :], 0.0) for i in range(slots)], axis=0
+    )
+    back_wide[...] = back.astype(jnp.bfloat16)
+    back_turned = back.T.astype(jnp.bfloat16)
+
+    @pl.loop(0, feats // step_cols)
+    def _(k):
+        cols = pl.ds(pl.multiple_of(k * step_cols, step_cols), step_cols)
+        dpart[r, :, cols] = adapter_scale * dot_nn(back_turned, act[:, cols])
+
+    r_down = remote(dpart.at[r], dpart.at[r], r_send.at[0], r_recv.at[0], to_r)
+    r_up = remote(upart.at[r], upart.at[r], r_send.at[1], r_recv.at[1], to_r)
+    r_down.start()
+    both(3)
+
+    @pl.loop(0, feats // step_cols)
+    def _(k):
+        cols = pl.ds(pl.multiple_of(k * step_cols, step_cols), step_cols)
+        igacc[:, cols] = dot_nn(dy_blocks[f], weights[f, :, cols]) + adapter_scale * dot_nn(
+            back_wide[...], down[:, cols]
+        )
+
+    both(4)
+    x_low_in.wait_recv()
+    total = low[0] + low[1]
+    in_wide[...] = total.astype(jnp.bfloat16)
+    turned = total.T.astype(jnp.bfloat16)
+    for q in range(2):
+        upart[r, :, q * block : (q + 1) * block] = adapter_scale * dot_nn(
+            turned, dy_blocks[2 * s + q]
+        )
+    r_up.start()
+    core_wait(0)
+    value_block(arrivals[0])
+    both(5)
+    grad_block(arrivals[0])
+    both(6)
+    remote(dpart.at[1 - r], dpart.at[1 - r], r_send.at[0], r_recv.at[0], to_r).wait_recv()
+    dsum[...] = (dpart[0] + dpart[1]).astype(jnp.bfloat16)
+    out_down = pltpu.make_async_copy(dsum, dgrad_h, out_sem.at[0])
+    out_down.start()
+    both(7)
+    remote(upart.at[1 - r], upart.at[1 - r], r_send.at[1], r_recv.at[1], to_r).wait_recv()
+    usum[...] = (upart[0] + upart[1]).astype(jnp.bfloat16)
+    out_up = pltpu.make_async_copy(usum, ugrad_h, out_sem.at[1])
+    out_up.start()
+    both(8)
+    core_wait(1)
+    value_block(arrivals[1])
+    both(9)
+    grad_block(arrivals[1])
+    both(10)
+    both(11)
+    y_step(11)
+    core_wait(2)
+    last = arrivals[2]
+    value_block(last)
+
+    def out_grad(k):
+        cols = pl.ds(pl.multiple_of(k * step_cols, step_cols), step_cols)
+        return pltpu.make_async_copy(igout.at[:, cols], igrad_h.at[:, cols], out_sem.at[3 + k])
+
+    @pl.loop(0, feats // step_cols)
+    def _(k):
+        cols = pl.ds(pl.multiple_of(k * step_cols, step_cols), step_cols)
+        igout[:, cols] = (igacc[:, cols] + dot_nn(dy_blocks[last], weights[last, :, cols])).astype(
+            jnp.bfloat16
+        )
+        out_grad(k).start()
+
+    for q in range(2):
+        v_copy(q).wait_recv()
+        extra = dot_nn(in_wide[...], up[s, :, q * block : (q + 1) * block])
+        for i in range(slots):
+            v = (
+                vpart[2 * s + q, tiles(i), :]
+                + vrecv[q, tiles(i), :].astype(jnp.float32)
+                + adapter_scale * extra[tiles(i), :]
+            )
+            vout[tiles(i), q * block : (q + 1) * block] = jnp.where(valid(i, block), v, 0.0).astype(
+                jnp.bfloat16
+            )
+    out_value = pltpu.make_async_copy(vout, value_h, out_sem.at[2])
+    out_value.start()
+
+    for c in range(CHUNKS):
+
+        @pl.when(f > 0)
+        def _():
+            own_copy(c, True).wait_send()
+
+        @pl.when(f < fsdp - 1)
+        def _():
+            own_copy(c, False).wait_send()
+
+        for j in arrivals:
+
+            @pl.when((j > f) & (f > 0))
+            def _():
+                z_copy(j, c, to_lo).wait_send()
+
+            @pl.when((j < f) & (f < fsdp - 1))
+            def _():
+                z_copy(j, c, to_hi).wait_send()
+
+            y_copy(j, c).wait_send()
+            ca_copy(j, c).wait_send()
+            cb_copy(j, c).wait_send()
+    x_dy.wait_send()
+    x_up.wait_send()
+    x_low.wait_send()
+    r_down.wait_send()
+    r_up.wait_send()
+    for q in range(2):
+        v_copy(q).wait_send()
+    for k in range(feats // step_cols):
+        out_grad(k).wait()
+    out_down.wait()
+    out_up.wait()
+    out_value.wait()
+
+
+def on_device(
+    activations,
+    cotangent,
+    base_weight,
+    adapter_down,
+    adapter_up,
+    tile_counts,
+    tile_length,
+    tile_adapter,
+):
+    rows, feats = activations.shape
+    heads = cotangent.shape[1]
+    sets, low_rank = adapter_up.shape[:2]
+    ranks = sets * low_rank
+    block = base_weight.shape[0]
+    down = adapter_down.transpose(0, 2, 1).reshape(ranks, feats)
+    up = adapter_up.reshape(ranks, heads)
+    bf16, f32 = jnp.bfloat16, jnp.float32
+    dma = pltpu.SemaphoreType.DMA
+    whole = pl.BlockSpec(memory_space=pl.ANY)
+    scalars = pl.BlockSpec(memory_space=pltpu.SMEM)
+    value, igrad, dgrad, ugrad = pl.pallas_call(
+        fused_kernel,
+        out_shape=(
+            jax.ShapeDtypeStruct((rows, heads), bf16),
+            jax.ShapeDtypeStruct((rows, feats), bf16),
+            jax.ShapeDtypeStruct((ranks, feats), bf16),
+            jax.ShapeDtypeStruct((ranks, heads), bf16),
+        ),
+        in_specs=[scalars] * 3 + [whole] * 5,
+        out_specs=(whole,) * 4,
+        scratch_shapes=[
+            pltpu.VMEM((rows, feats), bf16),
+            pltpu.VMEM((2, rows, heads), bf16),
+            pltpu.VMEM((4, rows, block), bf16),
+            pltpu.VMEM((4, block, feats), bf16),
+            pltpu.VMEM((ranks, feats), bf16),
+            pltpu.VMEM((2, ranks, heads), bf16),
+            pltpu.VMEM((2, rows, ranks), f32),
+            pltpu.VMEM((rows, ranks), bf16),
+            pltpu.VMEM((rows, ranks), bf16),
+            pltpu.VMEM((2, ranks, feats), f32),
+            pltpu.VMEM((ranks, feats), bf16),
+            pltpu.VMEM((2, ranks, heads), f32),
+            pltpu.VMEM((ranks, heads), bf16),
+            pltpu.VMEM((4, rows, block), f32),
+            pltpu.VMEM((2, rows, block), bf16),
+            pltpu.VMEM((2, rows, block), bf16),
+            pltpu.VMEM((rows, heads), bf16),
+            pltpu.VMEM((rows, feats), f32),
+            pltpu.VMEM((rows, feats), bf16),
+            dma((5,)),
+            dma((3 + feats // 512,)),
+            dma((2, CHUNKS)),
+        ]
+        + [dma((4, CHUNKS))] * 8
+        + [dma((3,)), dma((3,)), dma((2,)), dma((2,)), dma((2,)), dma((2,))],
+        compiler_params=pltpu.CompilerParams(
+            collective_id=0, has_side_effects=True, vmem_limit_bytes=60 * 1024 * 1024
+        ),
+    )(tile_counts, tile_length, tile_adapter, activations, cotangent, base_weight, down, up)
+    return (
+        value,
+        igrad,
+        dgrad.reshape(sets, low_rank, feats).transpose(0, 2, 1),
+        ugrad.reshape(sets, low_rank, heads),
+    )
+
+
 def solution(mesh):
+    sizes = (mesh.shape["groups"], mesh.shape["fsdp"], mesh.shape["sub"], mesh.shape["rep"])
     return jax.shard_map(
-        on_device,
+        on_device if sizes == (2, 4, 2, 2) else on_device_general,
         mesh=mesh,
         in_specs=(
             P(("groups", "fsdp", "rep"), "sub"),

time: 203 us -> 75.6 us (0.37)
  waiting for transfers between devices: 124 us -> 0 us
  Pallas kernels: 0 us -> 66 us
  blocking collectives: 31.5 us -> 0 us
  matrix products: 25.8 us -> 0 us
  between operations: 14.1 us -> 0.65 us
  local copies, waits for them, and re-layouts: 0.89 us -> 7.4 us
  other arithmetic: 3.5 us -> 0 us
    all_gather x1 -> x0, waiting for transfers between devices: 119 us -> none  [on_device(): whole_weight = lax.all_gather(base_weight, 'fsdp', axis=0, tiled=True)]
    pallas_call x0 -> x1, Pallas kernels: none -> 66 us  [on_device(): pl.pallas_call(fused_kernel, out_shape=(jax.ShapeDtypeStruct((rows, heads...]
    dot_general x8 -> x0, matrix products: 25.8 us -> none  [the longest x1 7.07 us: on_device(): lax.dot_general(activations, whole_weight, contract_last, preferred_eleme...]
    psum x2 -> x0, blocking collectives: 21 us -> none  [the longest x1 10.5 us: on_device(): down_total, up_total = lax.psum((down_grad, up_grad), 'rep')]
    all_gather x1 -> x0, blocking collectives: 10.6 us -> none  [on_device(): full_dy = lax.all_gather(work_dy, 'sub', axis=1, tiled=True)]
    unnamed x17 -> x8, local copies, waits for them, and re-layouts: 0.31 us -> 7.4 us
    reduce_scatter x1 -> x0, waiting for transfers between devices: 3.96 us -> none  [on_device(): lax.psum_scatter(value_part, 'sub', scatter_dimension=1, tiled=True)]
  transfers between devices with their start and end apart: 2 -> 0, of which waited for: 2 -> 0; matrix products, arithmetic and copies ran while one was open for 10% -> 0% of each run, Pallas kernels for 0% -> 0%
where the time goes in v1:
time: 75.6 us; the launch traced here: 74.1 us
  Pallas kernels  66 us (87%)
  local copies, waits for them, and re-layouts  7.4 us (10%)
    pallas_call x1, Pallas kernels, on_device(): pl.pallas_call(fused_kernel, out_shape=(jax.ShapeDtypeStruct((rows, heads...  66 us
    unnamed x8, local copies, waits for them, and re-layouts  7.4 us

profile of v1, /device:TPU:2, one launch (start us, length us, event | category | flops | bytes accessed | tf_op | source)
XLA Modules:
  0.0 74.1 jit_solution(15233761971345865849)
XLA Ops:
  0.6 66.0 %shard_map.111 = (bf16[384,512]{1,0:T(8,128)(2,1)}, bf16[384,4096]{1,0:T(8,128)(2,1)}, bf16[128,4096]{1,0:T(8,128)(2,1)}, bf16[128,512]{1,0:T(8,128)(2,1)}) custom-call(s32[8]{0:T(128)} %counts.1, s32[3]{0:T(128)} %lengths.1, s32[3]{0:T(128)} %picks.1, bf16[384,4096]{1,0:T(8,128)(2,1)} %act_h.1, bf16[384,512]{1,0:T(8,128)(2,1)} %dy_h.1, ...), custom_call_target="tpu_custom_call" | custom-call | tf_op jit(solution)/shard_map/pallas_call | solution.py:522
  66.7 1.8 %copy.16 = bf16[384,512]{1,0:T(8,128)(2,1)} copy(bf16[384,512]{1,0:T(8,128)(2,1)} %get-tuple-element.16) | data formatting | bytes 786432
  68.4 0.0 copy-start
  68.4 0.0 copy-start.1
  68.4 4.0 %copy.17 = bf16[384,4096]{1,0:T(8,128)(2,1)} copy(bf16[384,4096]{1,0:T(8,128)(2,1)} %get-tuple-element.17) | data formatting | bytes 6291456
  72.5 0.0 copy-done
  72.5 1.0 %copy.18 = bf16[2,4096,64]{1,2,0:T(8,128)(2,1)} copy(bf16[2,4096,64]{1,2,0:T(8,128)(2,1)S(1)} %bitcast.8) | data formatting | bytes 2097152
  73.4 0.0 copy-done.1
  73.4 0.7 copy.19
Async XLA Ops:
  68.4 4.0 %copy-start = (bf16[128,4096]{1,0:T(8,128)(2,1)S(1)}, bf16[128,4096]{1,0:T(8,128)(2,1)}, u32[]{:S(2)}) copy-start(bf16[128,4096]{1,0:T(8,128)(2,1)} %get-tuple-element.10) | copy-start | bytes 3145732
  68.4 5.0 %copy-start.1 = (bf16[128,512]{1,0:T(8,128)(2,1)S(1)}, bf16[128,512]{1,0:T(8,128)(2,1)}, u32[]{:S(2)}) copy-start(bf16[128,512]{1,0:T(8,128)(2,1)} %get-tuple-element.11) | copy-start | bytes 393220

commit v2 on v1

--- a/solution.py
+++ b/solution.py
@@ -340,8 +340,10 @@
 
     step_cols = 512
 
-    def grad_block(j):
-        @pl.loop(0, feats // step_cols)
+    half = feats // step_cols // 2
+
+    def grad_block(j, part):
+        @pl.loop(part * half, (part + 1) * half)
         def _(k):
             cols = pl.ds(pl.multiple_of(k * step_cols, step_cols), step_cols)
             igacc[:, cols] += dot_nn(dy_blocks[j], weights[j, :, cols])
@@ -390,15 +392,20 @@
     r_up = remote(upart.at[r], upart.at[r], r_send.at[1], r_recv.at[1], to_r)
     r_down.start()
     both(3)
-
-    @pl.loop(0, feats // step_cols)
-    def _(k):
-        cols = pl.ds(pl.multiple_of(k * step_cols, step_cols), step_cols)
-        igacc[:, cols] = dot_nn(dy_blocks[f], weights[f, :, cols]) + adapter_scale * dot_nn(
-            back_wide[...], down[:, cols]
-        )
-
     both(4)
+
+    def first_grad(part):
+        @pl.loop(part * half, (part + 1) * half)
+        def _(k):
+            cols = pl.ds(pl.multiple_of(k * step_cols, step_cols), step_cols)
+            igacc[:, cols] = dot_nn(dy_blocks[f], weights[f, :, cols]) + adapter_scale * dot_nn(
+                back_wide[...], down[:, cols]
+            )
+
+    first_grad(0)
+    both(5)
+    first_grad(1)
+    both(6)
     x_low_in.wait_recv()
     total = low[0] + low[1]
     in_wide[...] = total.astype(jnp.bfloat16)
@@ -410,26 +417,26 @@
     r_up.start()
     core_wait(0)
     value_block(arrivals[0])
-    both(5)
-    grad_block(arrivals[0])
-    both(6)
+    both(7)
+    grad_block(arrivals[0], 0)
+    both(8)
+    grad_block(arrivals[0], 1)
+    both(9)
+    core_wait(1)
+    value_block(arrivals[1])
+    both(10)
+    grad_block(arrivals[1], 0)
+    both(11)
+    grad_block(arrivals[1], 1)
+    y_step(11)
     remote(dpart.at[1 - r], dpart.at[1 - r], r_send.at[0], r_recv.at[0], to_r).wait_recv()
     dsum[...] = (dpart[0] + dpart[1]).astype(jnp.bfloat16)
     out_down = pltpu.make_async_copy(dsum, dgrad_h, out_sem.at[0])
     out_down.start()
-    both(7)
     remote(upart.at[1 - r], upart.at[1 - r], r_send.at[1], r_recv.at[1], to_r).wait_recv()
     usum[...] = (upart[0] + upart[1]).astype(jnp.bfloat16)
     out_up = pltpu.make_async_copy(usum, ugrad_h, out_sem.at[1])
     out_up.start()
-    both(8)
-    core_wait(1)
-    value_block(arrivals[1])
-    both(9)
-    grad_block(arrivals[1])
-    both(10)
-    both(11)
-    y_step(11)
     core_wait(2)
     last = arrivals[2]
     value_block(last)
@@ -496,6 +503,33 @@
     out_down.wait()
     out_up.wait()
     out_value.wait()
+
+
+def hand_on_kernel(*refs):
+    parts, count = 8, 4
+    sources, targets, held = refs[:count], refs[count : 2 * count], refs[2 * count : 3 * count]
+    into, out = refs[3 * count :]
+
+    def piece(i, k):
+        size = sources[i].shape[0] // parts
+        return pl.ds(k * size, size)
+
+    def load(i, k):
+        rows = piece(i, k)
+        return pltpu.make_async_copy(sources[i].at[rows], held[i].at[rows], into.at[i, k])
+
+    def store(i, k):
+        rows = piece(i, k)
+        return pltpu.make_async_copy(held[i].at[rows], targets[i].at[rows], out.at[i, k])
+
+    every = [(i, k) for i in range(count) for k in range(parts)]
+    for i, k in every:
+        load(i, k).start()
+    for i, k in every:
+        load(i, k).wait()
+        store(i, k).start()
+    for i, k in every:
+        store(i, k).wait()
 
 
 def on_device(
@@ -559,6 +593,15 @@
             collective_id=0, has_side_effects=True, vmem_limit_bytes=60 * 1024 * 1024
         ),
     )(tile_counts, tile_length, tile_adapter, activations, cotangent, base_weight, down, up)
+    results = (value, igrad, dgrad, ugrad)
+    value, igrad, dgrad, ugrad = pl.pallas_call(
+        hand_on_kernel,
+        out_shape=tuple(jax.ShapeDtypeStruct(a.shape, a.dtype) for a in results),
+        in_specs=[whole] * 4,
+        out_specs=(whole,) * 4,
+        scratch_shapes=[pltpu.VMEM(a.shape, a.dtype) for a in results] + [dma((4, 8)), dma((4, 8))],
+        compiler_params=pltpu.CompilerParams(vmem_limit_bytes=60 * 1024 * 1024),
+    )(*results)
     return (
         value,
         igrad,

time: 75.6 us -> 69.5 us (0.919); the launches traced: 74.1 us -> 69 us
  local copies, waits for them, and re-layouts: 7.4 us -> 0 us
  Pallas kernels: 66 us -> 68.3 us
    unnamed x8 -> x0, local copies, waits for them, and re-layouts: 7.4 us -> none
    pallas_call x0 -> x1, Pallas kernels: none -> 4.62 us  [on_device(): pl.pallas_call(hand_on_kernel, out_shape=tuple((jax.ShapeDtypeStruct(a.sh...]
    pallas_call x1, Pallas kernels: 66 us -> 63.7 us  [on_device(): pl.pallas_call(fused_kernel, out_shape=(jax.ShapeDtypeStruct((rows, heads...]
where the time goes in v2:
time: 69.5 us; the launch traced here: 69 us
  Pallas kernels  68.3 us (98%)
    pallas_call x1, Pallas kernels, on_device(): pl.pallas_call(fused_kernel, out_shape=(jax.ShapeDtypeStruct((rows, heads...  63.7 us
    pallas_call x1, Pallas kernels, on_device(): pl.pallas_call(hand_on_kernel, out_shape=tuple((jax.ShapeDtypeStruct(a.sh...  4.62 us

profile of v2, /device:TPU:2, one launch (start us, length us, event | category | flops | bytes accessed | tf_op | source)
XLA Modules:
  0.0 69.0 jit_solution(7718153408304589113)
XLA Ops:
  0.6 63.7 %shard_map.111 = (bf16[384,512]{1,0:T(8,128)(2,1)}, bf16[384,4096]{1,0:T(8,128)(2,1)}, bf16[128,4096]{1,0:T(8,128)(2,1)}, bf16[128,512]{1,0:T(8,128)(2,1)}) custom-call(s32[8]{0:T(128)} %counts.1, s32[3]{0:T(128)} %lengths.1, s32[3]{0:T(128)} %picks.1, bf16[384,4096]{1,0:T(8,128)(2,1)} %act_h.1, bf16[384,512]{1,0:T(8,128)(2,1)} %dy_h.1, ...), custom_call_target="tpu_custom_call" | custom-call | tf_op jit(solution)/shard_map/pallas_call | solution.py:556
  64.3 4.6 %shard_map.112 = (bf16[384,512]{1,0:T(8,128)(2,1)}, bf16[384,4096]{1,0:T(8,128)(2,1)}, bf16[128,4096]{1,0:T(8,128)(2,1)}, bf16[128,512]{1,0:T(8,128)(2,1)}) custom-call(bf16[384,512]{1,0:T(8,128)(2,1)} %get-tuple-element.12.refs_0_, bf16[384,4096]{1,0:T(8,128)(2,1)} %get-tuple-element.13.refs_1_, bf16[128,4096]{1,0:T(8,128)(2,1)} %get-tuple-element.14.refs_2_, ...), custom_call_target="tpu_custom_call" | custom-call | tf_op jit(solution)/shard_map/pallas_call | solution.py:597

commit v3 on v2

--- a/solution.py
+++ b/solution.py
@@ -304,13 +304,16 @@
         step(i)
         y_step(i - 1)
 
+    def core_wait_chunk(t, c):
+        j = arrivals[t]
+        here = piece(j, g, 1 - r, c)
+        remote(here, here, ca_send.at[j, c], ca_recv.at[j, c], to_r).wait_recv()
+        here = piece(j, 1 - g, 1 - r, c)
+        remote(here, here, cb_send.at[j, c], cb_recv.at[j, c], to_r).wait_recv()
+
     def core_wait(t):
-        j = arrivals[t]
         for c in range(CHUNKS):
-            here = piece(j, g, 1 - r, c)
-            remote(here, here, ca_send.at[j, c], ca_recv.at[j, c], to_r).wait_recv()
-            here = piece(j, 1 - g, 1 - r, c)
-            remote(here, here, cb_send.at[j, c], cb_recv.at[j, c], to_r).wait_recv()
+            core_wait_chunk(t, c)
 
     own_count = counts[f * 2 + r]
 
@@ -331,7 +334,9 @@
     def value_block(j):
         part = dot_nt(act[...], weights[j])
         vpart[j] = part
-
+        send_value(j, part)
+
+    def send_value(j, part):
         @pl.when(j // 2 != s)
         def _():
             q = j % 2
@@ -347,6 +352,31 @@
         def _(k):
             cols = pl.ds(pl.multiple_of(k * step_cols, step_cols), step_cols)
             igacc[:, cols] += dot_nn(dy_blocks[j], weights[j, :, cols])
+
+    last = arrivals[fsdp - 2]
+
+    def out_grad(p, c):
+        cols = pl.ds(p * quarter + c * width, width)
+        return pltpu.make_async_copy(
+            igout.at[:, cols], igrad_h.at[:, cols], out_sem.at[3 + p * CHUNKS + c]
+        )
+
+    def last_chunk(c):
+        core_wait_chunk(fsdp - 2, c)
+        part = vpart[last] if c > 0 else None
+        for p in range(4):
+            cols = slice(p * quarter + c * width, p * quarter + (c + 1) * width)
+            term = dot_nt(act[:, cols], weights[last, :, cols])
+            part = term if part is None else part + term
+        vpart[last] = part
+        if c == CHUNKS - 1:
+            send_value(last, part)
+        for p in range(4):
+            cols = slice(p * quarter + c * width, p * quarter + (c + 1) * width)
+            igout[:, cols] = (
+                igacc[:, cols] + dot_nn(dy_blocks[last], weights[last, :, cols])
+            ).astype(jnp.bfloat16)
+            out_grad(p, c).start()
 
     local[0].wait()
     local[1].wait()
@@ -354,9 +384,9 @@
     for i in range(slots):
         low[s, tiles(i), :] = jnp.where(chosen(i), wide[tiles(i), :], 0.0)
     x_low.start()
+    step(0)
     local[2].wait()
     value_block(f)
-    step(0)
     both(1)
     local[3].wait()
     local[4].wait()
@@ -428,7 +458,9 @@
     grad_block(arrivals[1], 0)
     both(11)
     grad_block(arrivals[1], 1)
+    last_chunk(0)
     y_step(11)
+    last_chunk(1)
     remote(dpart.at[1 - r], dpart.at[1 - r], r_send.at[0], r_recv.at[0], to_r).wait_recv()
     dsum[...] = (dpart[0] + dpart[1]).astype(jnp.bfloat16)
     out_down = pltpu.make_async_copy(dsum, dgrad_h, out_sem.at[0])
@@ -437,21 +469,8 @@
     usum[...] = (upart[0] + upart[1]).astype(jnp.bfloat16)
     out_up = pltpu.make_async_copy(usum, ugrad_h, out_sem.at[1])
     out_up.start()
-    core_wait(2)
-    last = arrivals[2]
-    value_block(last)
-
-    def out_grad(k):
-        cols = pl.ds(pl.multiple_of(k * step_cols, step_cols), step_cols)
-        return pltpu.make_async_copy(igout.at[:, cols], igrad_h.at[:, cols], out_sem.at[3 + k])
-
-    @pl.loop(0, feats // step_cols)
-    def _(k):
-        cols = pl.ds(pl.multiple_of(k * step_cols, step_cols), step_cols)
-        igout[:, cols] = (igacc[:, cols] + dot_nn(dy_blocks[last], weights[last, :, cols])).astype(
-            jnp.bfloat16
-        )
-        out_grad(k).start()
+    last_chunk(2)
+    last_chunk(3)
 
     for q in range(2):
         v_copy(q).wait_recv()
@@ -498,8 +517,9 @@
     r_up.wait_send()
     for q in range(2):
         v_copy(q).wait_send()
-    for k in range(feats // step_cols):
-        out_grad(k).wait()
+    for p in range(4):
+        for c in range(CHUNKS):
+            out_grad(p, c).wait()
     out_down.wait()
     out_up.wait()
     out_value.wait()
@@ -584,7 +604,7 @@
             pltpu.VMEM((rows, feats), f32),
             pltpu.VMEM((rows, feats), bf16),
             dma((5,)),
-            dma((3 + feats // 512,)),
+            dma((3 + 4 * CHUNKS,)),
             dma((2, CHUNKS)),
         ]
         + [dma((4, CHUNKS))] * 8

time: 69.5 us -> 69.5 us (level)
  no operation moved by 1% of the time
where the time goes in v3:
time: 69.5 us; the launch traced here: 69.3 us
  Pallas kernels  68.7 us (99%)
    pallas_call x1, Pallas kernels, on_device(): pl.pallas_call(fused_kernel, out_shape=(jax.ShapeDtypeStruct((rows, heads...  64.1 us
    pallas_call x1, Pallas kernels, on_device(): pl.pallas_call(hand_on_kernel, out_shape=tuple((jax.ShapeDtypeStruct(a.sh...  4.62 us

profile of v3, /device:TPU:2, one launch (start us, length us, event | category | flops | bytes accessed | tf_op | source)
XLA Modules:
  0.0 69.3 jit_solution(13440186606240243342)
XLA Ops:
  0.6 64.1 %shard_map.111 = (bf16[384,512]{1,0:T(8,128)(2,1)}, bf16[384,4096]{1,0:T(8,128)(2,1)}, bf16[128,4096]{1,0:T(8,128)(2,1)}, bf16[128,512]{1,0:T(8,128)(2,1)}) custom-call(s32[8]{0:T(128)} %counts.1, s32[3]{0:T(128)} %lengths.1, s32[3]{0:T(128)} %picks.1, bf16[384,4096]{1,0:T(8,128)(2,1)} %act_h.1, bf16[384,512]{1,0:T(8,128)(2,1)} %dy_h.1, ...), custom_call_target="tpu_custom_call" | custom-call | tf_op jit(solution)/shard_map/pallas_call | solution.py:576
  64.7 4.6 %shard_map.112 = (bf16[384,512]{1,0:T(8,128)(2,1)}, bf16[384,4096]{1,0:T(8,128)(2,1)}, bf16[128,4096]{1,0:T(8,128)(2,1)}, bf16[128,512]{1,0:T(8,128)(2,1)}) custom-call(bf16[384,512]{1,0:T(8,128)(2,1)} %get-tuple-element.12.refs_0_, bf16[384,4096]{1,0:T(8,128)(2,1)} %get-tuple-element.13.refs_1_, bf16[128,4096]{1,0:T(8,128)(2,1)} %get-tuple-element.14.refs_2_, ...), custom_call_target="tpu_custom_call" | custom-call | tf_op jit(solution)/shard_map/pallas_call | solution.py:617

commit v4 on v3

--- a/solution.py
+++ b/solution.py
@@ -236,8 +236,7 @@
             to_lo if down_way else to_hi,
         )
 
-    for c in range(CHUNKS):
-
+    def own_start(c):
         @pl.when(f > 0)
         def _():
             own_copy(c, True).start()
@@ -245,6 +244,9 @@
         @pl.when(f < fsdp - 1)
         def _():
             own_copy(c, False).start()
+
+    own_start(0)
+    own_start(1)
 
     x_dy = remote(dy_h, dy_raw.at[s], x_send.at[0], x_recv.at[0], to_x)
     x_up = remote(up_h, up.at[s], x_send.at[1], x_recv.at[1], to_x)
@@ -385,9 +387,11 @@
         low[s, tiles(i), :] = jnp.where(chosen(i), wide[tiles(i), :], 0.0)
     x_low.start()
     step(0)
+    own_start(2)
     local[2].wait()
     value_block(f)
     both(1)
+    own_start(3)
     local[3].wait()
     local[4].wait()
     x_dy_in = remote(dy_raw.at[1 - s], dy_raw.at[1 - s], x_send.at[0], x_recv.at[0], to_x)

time: 69.5 us -> 69.6 us (level)
  no operation moved by 1% of the time
where the time goes in v4:
time: 69.6 us; the launch traced here: 69.4 us
  Pallas kernels  68.8 us (99%)
    pallas_call x1, Pallas kernels, on_device(): pl.pallas_call(fused_kernel, out_shape=(jax.ShapeDtypeStruct((rows, heads...  64.2 us
    pallas_call x1, Pallas kernels, on_device(): pl.pallas_call(hand_on_kernel, out_shape=tuple((jax.ShapeDtypeStruct(a.sh...  4.62 us

profile of v4, /device:TPU:2, one launch (start us, length us, event | category | flops | bytes accessed | tf_op | source)
XLA Modules:
  0.0 69.4 jit_solution(15379060104024803026)
XLA Ops:
  0.6 64.2 %shard_map.111 = (bf16[384,512]{1,0:T(8,128)(2,1)}, bf16[384,4096]{1,0:T(8,128)(2,1)}, bf16[128,4096]{1,0:T(8,128)(2,1)}, bf16[128,512]{1,0:T(8,128)(2,1)}) custom-call(s32[8]{0:T(128)} %counts.1, s32[3]{0:T(128)} %lengths.1, s32[3]{0:T(128)} %picks.1, bf16[384,4096]{1,0:T(8,128)(2,1)} %act_h.1, bf16[384,512]{1,0:T(8,128)(2,1)} %dy_h.1, ...), custom_call_target="tpu_custom_call" | custom-call | tf_op jit(solution)/shard_map/pallas_call | solution.py:580
  64.8 4.6 %shard_map.112 = (bf16[384,512]{1,0:T(8,128)(2,1)}, bf16[384,4096]{1,0:T(8,128)(2,1)}, bf16[128,4096]{1,0:T(8,128)(2,1)}, bf16[128,512]{1,0:T(8,128)(2,1)}) custom-call(bf16[384,512]{1,0:T(8,128)(2,1)} %get-tuple-element.12.refs_0_, bf16[384,4096]{1,0:T(8,128)(2,1)} %get-tuple-element.13.refs_1_, bf16[128,4096]{1,0:T(8,128)(2,1)} %get-tuple-element.14.refs_2_, ...), custom_call_target="tpu_custom_call" | custom-call | tf_op jit(solution)/shard_map/pallas_call | solution.py:621
